TPU v7x, 32 devices: a whole 2x2x4 slice. The times are simulated.
32 devices in a mesh: py: 4 (over z), pz: 8 (over y, x, core).
Axes of the slice: x: 2, y: 2, z: 4, core: 2. Of those that a mesh axis runs over, the one named last changes fastest.
Arguments:
- vort_p: bfloat16 [3, 131072], P(None, ('py', 'pz')), may hold values from -6 to 6
- pair_weights: bfloat16 [8192, 64, 128], P(('py', 'pz')), may hold values from -1.796875 to 1.796875
- pair_part: int32 [8192], P(('py', 'pz')), may hold values from 0 to 31
- pair_node: int32 [8192], P(('py', 'pz')), may hold values from 0 to 95, as said below
- counts: int32 [32], P(('py', 'pz')), may hold values from 128 to 256, as said below
Outputs:
- vel_p: float32 [3, 131072], P(None, ('py', 'pz'))
Inputs may be any that keep to these rules, and one draw needn't show every extreme that they name: `counts`: every pencil has at least 128 live slots, and some pencil has all 256 slots live in every draw. `pair_node`: in every pencil the slots below 96 name each of its node blocks exactly once.
All inputs are finite; a program needn't handle non-finite values.
Results may differ from a plain program's by a relative error of at most 0.0029.
Values sent between devices are 32-bit elements; how exact they have to be, the bound alone decides.
A program may use at most 64 MiB of HBM per device.

v0:
```python
import math
import jax
import jax.numpy as jnp
from jax import lax
from jax.sharding import PartitionSpec as P

NX = 384
CY = 8
CZ = 2
BP = 128
BN = 64
PB_DEV = 32


def twiddle(row_index, col_index, period):
    product = row_index[:, None] * col_index[None, :] % period
    return product.astype(jnp.float32) * (2.0 * math.pi / period)


def forward_table(length):
    angle = twiddle(jnp.arange(length), jnp.arange(length), length)
    cosine = jnp.cos(angle)
    sines = jnp.sin(angle)
    return jnp.stack([jnp.stack([cosine, -sines], 1), jnp.stack([sines, cosine], 1)], 0)


def inverse_table(length):
    angle = twiddle(jnp.arange(length), jnp.arange(length), length)
    cosine = jnp.cos(angle) / length
    sines = jnp.sin(angle) / length
    return jnp.stack([jnp.stack([cosine, sines], 1), jnp.stack([-sines, cosine], 1)], 0)


def cross_terms(coeffs, field):
    return jnp.stack(
        [
            coeffs[1] * field[2] - coeffs[2] * field[1],
            coeffs[2] * field[0] - coeffs[0] * field[2],
            coeffs[0] * field[1] - coeffs[1] * field[0],
        ],
        axis=0,
    )


def signed_wave(length, index):
    signed = jnp.where(index < length // 2, index, index - length)
    return (signed.astype(jnp.float32) * (2.0 * math.pi / length), index == length // 2)


def curl_solve(spectrum, y_cells, z_cells):
    x_local = spectrum.shape[1]
    y_local = spectrum.shape[3]
    mode_x = lax.axis_index("py") * x_local + jnp.arange(x_local)
    wave_x = mode_x.astype(jnp.float32) * (2.0 * math.pi / NX)
    wave_y, edge_y = signed_wave(y_cells, lax.axis_index("pz") * y_local + jnp.arange(y_local))
    wave_z, edge_z = signed_wave(z_cells, jnp.arange(z_cells))
    wave_x3 = wave_x[:, None, None]
    wave_y3 = wave_y[None, :, None]
    wave_z3 = wave_z[None, None, :]
    total = wave_x3 * wave_x3 + wave_y3 * wave_y3 + wave_z3 * wave_z3
    edges = edge_y[None, :, None] | edge_z[None, None, :]
    keep = (total > 0) & jnp.logical_not(edges)
    inverse_sq = jnp.where(keep, 1.0 / jnp.where(keep, total, 1.0), 0.0)
    inv_wave = (wave_x3 * inverse_sq, wave_y3 * inverse_sq, wave_z3 * inverse_sq)
    real_turn = cross_terms(inv_wave, spectrum[:, :, 0])
    imag_turn = cross_terms(inv_wave, spectrum[:, :, 1])
    return jnp.stack([-imag_turn, real_turn], axis=2)


def per_device(vort_p, pair_weights, pair_part, pair_node, counts):
    highest = lax.Precision.HIGHEST
    y_cells = CY * lax.axis_size("py")
    z_cells = CZ * lax.axis_size("pz")
    x_modes = NX // 2
    node_blocks = NX * CY * CZ // BN
    pair_slots = pair_weights.shape[0]
    live_mask = (jnp.arange(pair_slots) < counts[0]).astype(jnp.float32)
    particle_blocks = vort_p.reshape(3, PB_DEV, BP).transpose(1, 0, 2)
    picked = particle_blocks[pair_part]
    products = jnp.einsum("pcq,pnq->pcn", picked, pair_weights, preferred_element_type=jnp.float32)
    products = products * live_mask[:, None, None]
    node_sums = jax.ops.segment_sum(products, pair_node, num_segments=node_blocks)
    vort_grid = node_sums.transpose(1, 0, 2).reshape(3, CZ, CY, NX)
    angle_fwd = twiddle(jnp.arange(NX), jnp.arange(x_modes), NX)
    x_forward = jnp.stack([jnp.cos(angle_fwd), -jnp.sin(angle_fwd)], 1)
    angle_inv = twiddle(jnp.arange(x_modes), jnp.arange(NX), NX)
    mode_weight = (jnp.where(jnp.arange(x_modes) == 0, 1.0, 2.0) / NX)[:, None]
    x_inverse = jnp.stack([mode_weight * jnp.cos(angle_inv), -mode_weight * jnp.sin(angle_inv)], 0)
    y_forward = forward_table(y_cells)
    z_forward = forward_table(z_cells)
    z_inverse = inverse_table(z_cells)
    y_inverse = inverse_table(y_cells)
    x_spectrum = jnp.einsum("czyx,xrm->czrmy", vort_grid, x_forward, precision=highest)
    row_section = jnp.einsum(
        "czrmy,rysk->cmskz",
        lax.all_to_all(x_spectrum, "py", split_axis=3, concat_axis=4, tiled=True),
        y_forward,
        precision=highest,
    )
    col_section = jnp.einsum(
        "cmrkz,rzsw->cmskw",
        lax.all_to_all(row_section, "pz", split_axis=3, concat_axis=4, tiled=True),
        z_forward,
        precision=highest,
    )
    vel_spectrum = curl_solve(col_section, y_cells, z_cells)
    z_back = jnp.einsum("cmrkw,rwsz->cmszk", vel_spectrum, z_inverse, precision=highest)
    y_back = jnp.einsum(
        "cmrzk,rksy->czsym",
        lax.all_to_all(z_back, "pz", split_axis=3, concat_axis=4, tiled=True),
        y_inverse,
        precision=highest,
    )
    vel_grid = jnp.einsum(
        "czrym,rmx->czyx",
        lax.all_to_all(y_back, "py", split_axis=3, concat_axis=4, tiled=True),
        x_inverse,
        precision=highest,
    )
    vel_nodes = vel_grid.astype(jnp.bfloat16).reshape(3, node_blocks, BN).transpose(1, 0, 2)
    chosen = vel_nodes[pair_node]
    back_products = jnp.einsum(
        "pcn,pnq->pcq", chosen, pair_weights, preferred_element_type=jnp.float32
    )
    back_products = back_products * live_mask[:, None, None]
    block_sums = jax.ops.segment_sum(back_products, pair_part, num_segments=PB_DEV)
    return block_sums.transpose(1, 0, 2).reshape(3, PB_DEV * BP)


def solution(mesh):
    placed = (
        P(None, ("py", "pz")),
        P(("py", "pz"), None, None),
        P(("py", "pz")),
        P(("py", "pz")),
        P(("py", "pz")),
    )
    return jax.shard_map(
        per_device, mesh=mesh, in_specs=placed, out_specs=P(None, ("py", "pz")), check_vma=False
    )
```

profile of v0, /device:TPU:0, one launch (start us, length us, event | category | flops | bytes accessed | tf_op | source)
XLA Modules:
  0.0 85.7 jit_solution(18046302165905745508)
XLA Ops:
  0.0 1.2 %sine_negate_fusion = (f32[384,1,192]{0,2,1:T(8,128)S(1)}, f32[384,1,192]{0,2,1:T(8,128)S(1)}) fusion(), kind=kLoop, calls=%fused_computation.30 | loop fusion | flops 737280 | bytes 589824 | tf_op jit(solution)/shard_map/neg | solution.py:85
  1.9 0.7 compare_select_fusion.1
  2.6 1.0 %gather_fusion = bf16[256,3,128]{2,1,0:T(4,128)(2,1)S(1)} fusion(bf16[32,3,128]{2,1,0:T(4,128)(2,1)S(1)} %bitcast.162, s32[1024]{0:T(1024)S(1)} %pad_clamp_fusion.1), kind=kCustom, calls=%fused_computation | custom fusion | bytes 394240 | tf_op jit(solution)/shard_map/gather | solution.py:79
  3.6 4.4 %convolution_multiply_fusion.1 = f32[256,3,64]{2,1,0:T(4,128)S(1)} fusion(bf16[256,3,128]{2,1,0:T(4,128)(2,1)S(1)} %gather_fusion, bf16[256,64,128]{2,1,0:T(8,128)(2,1)} %param.6, f32[256]{0:T(256)S(1)} %compare_convert_fusion), kind=kOutput, calls=%fused_computation.5 | convolution fusion | flops 12632064 | bytes 4588544 | tf_op jit(solution)/shard_map/pcq,pnq->pcn/dot_general | solution.py:80
  8.1 8.3 %scatter_fusion = f32[96,3,64]{2,1,0:T(4,128)S(1)} fusion(f32[96,3,64]{2,1,0:T(4,128)S(1)} %broadcast_in_dim.24, s32[256]{0:T(256)S(1)} %copy-done.2, f32[256,3,64]{2,1,0:T(4,128)S(1)} %convolution_multiply_fusion.1), kind=kCustom, calls=%fused_computation.2 | custom fusion | flops 49152 | bytes 590848 | tf_op jit(solution)/shard_map/scatter-add | solution.py:82
  16.4 0.1 reshape.719
  16.5 0.9 %convolution_bitcast_fusion.4 = f32[3,2,2,192,8]{3,4,1,0,2:T(8,128)S(1)} fusion(f32[3,2,8,384,1]{3,2,1,0,4:T(8,128)S(1)} %reshape.719, f32[384,1,192]{0,2,1:T(8,128)S(1)} %get-tuple-element.19, f32[384,1,192]{0,2,1:T(8,128)S(1)} %get-tuple-element.20), kind=kOutput, calls=%fused_computation.10 | convolution fusion | flops 85082112 | bytes 737280 | tf_op jit(solution)/shard_map/czyx,xrm->czrmy/dot_general | solution.py:93
  17.4 0.8 copy.33
  18.2 2.5 %reshape.735 = f32[4,1,4608]{2,1,0:T(1,128)} reshape(f32[192,2,3,2,8]{4,3,2,1,0:T(2,128)S(1)} %bitcast.163) | data formatting | bytes 147456
  20.7 6.3 %all-to-all-start = ((f32[4,1,4608]{2,1,0:T(1,128)}), f32[4,1,4608]{2,1,0:T(1,128)S(1)}, u32[]{:S(2)}, u32[]{:S(2)}) async-start(f32[4,1,4608]{2,1,0:T(1,128)} %reshape.735), calls=%async_computation | async-start | bytes 147456 | tf_op jit(solution)/shard_map/all_to_all | solution.py:96
  27.5 0.1 broadcast_multiply_fusion
  27.8 1.2 %sine_multiply_fusion = (f32[1,192,384]{2,1,0:T(8,128)S(1)}, f32[1,192,384]{2,1,0:T(8,128)S(1)}) fusion(f32[192]{0:T(256)S(1)} %fusion.57, f32[192]{0:T(256)S(1)} %fusion.51), kind=kLoop, calls=%fused_computation.25 | loop fusion | flops 811008 | bytes 591360 | tf_op jit(solution)/shard_map/mul | solution.py:88
  29.2 3.6 %all-to-all-done = f32[4,1,4608]{2,1,0:T(1,128)S(1)} async-done(((f32[4,1,4608]{2,1,0:T(1,128)}), f32[4,1,4608]{2,1,0:T(1,128)S(1)}, u32[]{:S(2)}, u32[]{:S(2)}) %all-to-all-start) | async-done | bytes 73760 | tf_op jit(solution)/shard_map/all_to_all | solution.py:96
  32.8 0.5 broadcast.1152
  33.3 0.8 reduce
  34.1 1.8 %reshape.736 = f32[192,2,3,2,8]{4,3,2,1,0:T(2,128)S(1)} reshape(f32[4,4608]{1,0:T(4,128)S(1)} %reduce) | data formatting | bytes 147456
  35.9 0.7 copy.34
  36.6 0.4 convolution_bitcast_fusion.3
  37.0 0.2 copy.81
  37.2 1.0 %reshape.737 = f32[8,1,2304]{2,1,0:T(1,128)} reshape(f32[32,2,3,2,48]{4,3,2,1,0:T(2,128)S(1)} %bitcast.168) | data formatting | bytes 147456
  38.1 3.7 %all-to-all-start.1 = ((f32[8,1,2304]{2,1,0:T(1,128)}), f32[8,1,2304]{2,1,0:T(1,128)S(1)}, u32[]{:S(2)}, u32[]{:S(2)}) async-start(f32[8,1,2304]{2,1,0:T(1,128)} %reshape.737), calls=%async_computation.1 | async-start | bytes 147456 | tf_op jit(solution)/shard_map/all_to_all | solution.py:102
  41.8 5.1 %all-to-all-done.1 = f32[8,1,2304]{2,1,0:T(1,128)S(1)} async-done(((f32[8,1,2304]{2,1,0:T(1,128)}), f32[8,1,2304]{2,1,0:T(1,128)S(1)}, u32[]{:S(2)}, u32[]{:S(2)}) %all-to-all-start.1) | async-done | bytes 73760 | tf_op jit(solution)/shard_map/all_to_all | solution.py:102
  46.9 0.8 reduce.1
  47.7 0.3 reshape.738
  48.2 0.4 convolution_bitcast_fusion.2
  48.5 0.1 multiply_subtract_fusion.5
  48.6 0.1 multiply_subtract_fusion.2
  48.8 0.4 convolution_bitcast_fusion.1
  49.3 0.9 %reshape.739 = f32[8,1,2304]{2,1,0:T(1,128)} reshape(f32[16,2,3,4,48]{4,3,2,1,0:T(4,128)S(1)} %bitcast.170) | data formatting | bytes 147456
  50.1 3.5 %all-to-all-start.2 = ((f32[8,1,2304]{2,1,0:T(1,128)}), f32[8,1,2304]{2,1,0:T(1,128)S(1)}, u32[]{:S(2)}, u32[]{:S(2)}) async-start(f32[8,1,2304]{2,1,0:T(1,128)} %reshape.739), calls=%async_computation.2 | async-start | bytes 147456 | tf_op jit(solution)/shard_map/all_to_all | solution.py:110
  53.7 4.8 %all-to-all-done.2 = f32[8,1,2304]{2,1,0:T(1,128)S(1)} async-done(((f32[8,1,2304]{2,1,0:T(1,128)}), f32[8,1,2304]{2,1,0:T(1,128)S(1)}, u32[]{:S(2)}, u32[]{:S(2)}) %all-to-all-start.2) | async-done | bytes 73760 | tf_op jit(solution)/shard_map/all_to_all | solution.py:110
  58.5 0.8 reduce.2
  59.3 0.2 reshape.740
  59.5 0.4 convolution_bitcast_fusion
  59.9 0.2 copy.79
  60.1 1.0 %reshape.741 = f32[4,1,4608]{2,1,0:T(1,128)} reshape(f32[32,2,3,2,48]{4,3,2,1,0:T(2,128)S(1)} %bitcast.172) | data formatting | bytes 147456
  61.0 3.3 %all-to-all-start.3 = ((f32[4,1,4608]{2,1,0:T(1,128)}), f32[4,1,4608]{2,1,0:T(1,128)S(1)}, u32[]{:S(2)}, u32[]{:S(2)}) async-start(f32[4,1,4608]{2,1,0:T(1,128)} %reshape.741), calls=%async_computation.3 | async-start | bytes 147456 | tf_op jit(solution)/shard_map/all_to_all | solution.py:116
  64.4 5.7 %all-to-all-done.3 = f32[4,1,4608]{2,1,0:T(1,128)S(1)} async-done(((f32[4,1,4608]{2,1,0:T(1,128)}), f32[4,1,4608]{2,1,0:T(1,128)S(1)}, u32[]{:S(2)}, u32[]{:S(2)}) %all-to-all-start.3) | async-done | bytes 73760 | tf_op jit(solution)/shard_map/all_to_all | solution.py:116
  70.1 0.8 reduce.3
  70.9 0.3 reshape.742
  71.3 0.1 copy.77
  71.4 0.1 all_to_all.67
  71.5 0.5 fusion
  72.0 0.1 reshape.680
  72.2 1.0 %gather_fusion.1 = bf16[256,3,64]{2,1,0:T(4,128)(2,1)S(1)} fusion(bf16[96,3,64]{2,1,0:T(4,128)(2,1)S(1)} %bitcast.166, s32[1024]{0:T(1024)S(1)} %pad_clamp_fusion), kind=kCustom, calls=%fused_computation.1 | custom fusion | bytes 197632 | tf_op jit(solution)/shard_map/gather | solution.py:121
  73.2 3.4 %convolution_multiply_fusion = f32[256,3,128]{2,1,0:T(4,128)S(1)} fusion(bf16[256,3,64]{2,1,0:T(4,128)(2,1)S(1)} %gather_fusion.1, bf16[256,64,128]{2,1,0:T(8,128)(2,1)} %param.6, f32[256]{0:T(256)S(1)} %compare_convert_fusion), kind=kOutput, calls=%fused_computation.4 | convolution fusion | flops 12681216 | bytes 4686848 | tf_op jit(solution)/shard_map/pcn,pnq->pcq/dot_general | solution.py:122
  76.6 8.4 %scatter_fusion.1 = f32[32,3,128]{2,1,0:T(4,128)S(1)} fusion(f32[32,3,128]{2,1,0:T(4,128)S(1)} %broadcast_in_dim.22, s32[256]{0:T(256)S(1)} %copy-done.3, f32[256,3,128]{2,1,0:T(4,128)S(1)} %convolution_multiply_fusion), kind=kCustom, calls=%fused_computation.3 | custom fusion | flops 98304 | bytes 1180672 | tf_op jit(solution)/shard_map/scatter-add | solution.py:126
  85.1 0.6 copy-done.1
  (40 shorter events, 1.1 us)
Async XLA Ops:
  0.0 2.6 %copy-start = (bf16[3,4096]{1,0:T(4,128)(2,1)S(1)}, bf16[3,4096]{1,0:T(4,128)(2,1)}, u32[]{:S(2)}) copy-start(bf16[3,4096]{1,0:T(4,128)(2,1)} %param.5) | copy-start | bytes 73732
  0.0 8.1 %copy-start.2 = (s32[256]{0:T(256)S(1)}, s32[256]{0:T(256)}, u32[]{:S(2)}) copy-start(s32[256]{0:T(256)} %param.8) | copy-start | bytes 3076
  20.7 12.1 %all-to-all-start = ((f32[4,1,4608]{2,1,0:T(1,128)}), f32[4,1,4608]{2,1,0:T(1,128)S(1)}, u32[]{:S(2)}, u32[]{:S(2)}) async-start(f32[4,1,4608]{2,1,0:T(1,128)} %reshape.735), calls=%async_computation | async-start | bytes 147456 | tf_op jit(solution)/shard_map/all_to_all | solution.py:96
  38.1 8.8 %all-to-all-start.1 = ((f32[8,1,2304]{2,1,0:T(1,128)}), f32[8,1,2304]{2,1,0:T(1,128)S(1)}, u32[]{:S(2)}, u32[]{:S(2)}) async-start(f32[8,1,2304]{2,1,0:T(1,128)} %reshape.737), calls=%async_computation.1 | async-start | bytes 147456 | tf_op jit(solution)/shard_map/all_to_all | solution.py:102
  50.1 8.4 %all-to-all-start.2 = ((f32[8,1,2304]{2,1,0:T(1,128)}), f32[8,1,2304]{2,1,0:T(1,128)S(1)}, u32[]{:S(2)}, u32[]{:S(2)}) async-start(f32[8,1,2304]{2,1,0:T(1,128)} %reshape.739), calls=%async_computation.2 | async-start | bytes 147456 | tf_op jit(solution)/shard_map/all_to_all | solution.py:110
  59.9 16.7 %copy-start.3 = (s32[256]{0:T(256)S(1)}, s32[256]{0:T(256)}, u32[]{:S(2)}) copy-start(s32[256]{0:T(256)} %param.7) | copy-start | bytes 3076
  61.0 9.0 %all-to-all-start.3 = ((f32[4,1,4608]{2,1,0:T(1,128)}), f32[4,1,4608]{2,1,0:T(1,128)S(1)}, u32[]{:S(2)}, u32[]{:S(2)}) async-start(f32[4,1,4608]{2,1,0:T(1,128)} %reshape.741), calls=%async_computation.3 | async-start | bytes 147456 | tf_op jit(solution)/shard_map/all_to_all | solution.py:116
  85.1 0.6 copy-start.1
where the time goes:
time: 86.3 us; the launch traced here: 85.7 us
  other arithmetic  24.3 us (28%)
  waiting for transfers between devices  19.2 us (22%)
  starting transfers between devices  16.9 us (20%)
  local copies, waits for them, and re-layouts  13.6 us (16%)
  matrix products  10.6 us (12%)
  between operations  1.09 us (1%)
    unnamed x16, local copies, waits for them, and re-layouts  8.58 us
    scatter-add x1, other arithmetic, per_device(): jax.ops.segment_sum(back_products, pair_part, num_segments=PB_DEV)  8.45 us
    scatter-add x1, other arithmetic, per_device(): jax.ops.segment_sum(products, pair_node, num_segments=node_blocks)  8.34 us
    all_to_all x1, starting transfers between devices, per_device(): lax.all_to_all(x_spectrum, 'py', split_axis=3, concat_axis=4, tiled=True)  6.33 us
    all_to_all x1, waiting for transfers between devices, per_device(): lax.all_to_all(y_back, 'py', split_axis=3, concat_axis=4, tiled=True)  5.72 us
    all_to_all x1, waiting for transfers between devices, per_device(): lax.all_to_all(row_section, 'pz', split_axis=3, concat_axis=4, tiled=True)  5.05 us
    all_to_all x1, waiting for transfers between devices, per_device(): lax.all_to_all(z_back, 'pz', split_axis=3, concat_axis=4, tiled=True)  4.8 us
    dot_general x1, matrix products, per_device(): jnp.einsum('pcq,pnq->pcn', picked, pair_weights, preferred_element_type=j...  4.45 us
  transfers between devices with their start and end apart: 4, of which 4 were waited for; matrix products, arithmetic and copies ran while one was open for 2% of the time, Pallas kernels for 0%

commit v1 on v0

--- a/solution.py
+++ b/solution.py
@@ -10,6 +10,15 @@
 BP = 128
 BN = 64
 PB_DEV = 32
+
+
+def step_on_widths(xx, lane_axis):
+    return jnp.concatenate(
+        jax.lax.all_to_all(
+            jnp.stack(jnp.split(xx, jax.lax.axis_size(lane_axis), axis=3)), lane_axis, 0, 0
+        ),
+        axis=4,
+    )
 
 
 def twiddle(row_index, col_index, period):
@@ -98,10 +107,7 @@
         precision=highest,
     )
     col_section = jnp.einsum(
-        "cmrkz,rzsw->cmskw",
-        lax.all_to_all(row_section, "pz", split_axis=3, concat_axis=4, tiled=True),
-        z_forward,
-        precision=highest,
+        "cmrkz,rzsw->cmskw", step_on_widths(row_section, "pz"), z_forward, precision=highest
     )
     vel_spectrum = curl_solve(col_section, y_cells, z_cells)
     z_back = jnp.einsum("cmrkw,rwsz->cmszk", vel_spectrum, z_inverse, precision=highest)

time: 86.3 us -> 86.9 us (level)
    all_to_all x1, waiting for transfers between devices: 5.72 us -> 4.31 us  [per_device(): lax.all_to_all(y_back, 'py', split_axis=3, concat_axis=4, tiled=True)]
    all_to_all x1, waiting for transfers between devices: 3.62 us -> 4.87 us  [per_device(): lax.all_to_all(x_spectrum, 'py', split_axis=3, concat_axis=4, tiled=True)]
    unnamed x16 -> x23, local copies, waits for them, and re-layouts: 8.58 us -> 8.44 us
where the time goes in v1:
time: 86.9 us; the launch traced here: 86.3 us
  other arithmetic  24.9 us (29%)
  waiting for transfers between devices  19.2 us (22%)
  starting transfers between devices  17 us (20%)
  local copies, waits for them, and re-layouts  13.4 us (15%)
  matrix products  10.6 us (12%)
  between operations  1.13 us (1%)
    scatter-add x1, other arithmetic, per_device(): jax.ops.segment_sum(back_products, pair_part, num_segments=PB_DEV)  8.45 us
    unnamed x23, local copies, waits for them, and re-layouts  8.44 us
    scatter-add x1, other arithmetic, per_device(): jax.ops.segment_sum(products, pair_node, num_segments=node_blocks)  8.34 us
    all_to_all x1, starting transfers between devices, per_device(): lax.all_to_all(x_spectrum, 'py', split_axis=3, concat_axis=4, tiled=True)  6.33 us
    all_to_all x1, waiting for transfers between devices, step_on_widths(): jax.lax.all_to_all(jnp.stack(jnp.split(xx, jax.lax.axis_size(lane_axis),...  5.06 us
    all_to_all x1, waiting for transfers between devices, per_device(): lax.all_to_all(z_back, 'pz', split_axis=3, concat_axis=4, tiled=True)  4.98 us
    all_to_all x1, waiting for transfers between devices, per_device(): lax.all_to_all(x_spectrum, 'py', split_axis=3, concat_axis=4, tiled=True)  4.87 us
    dot_general x1, matrix products, per_device(): jnp.einsum('pcq,pnq->pcn', picked, pair_weights, preferred_element_type=j...  4.45 us
  transfers between devices with their start and end apart: 4, of which 4 were waited for; matrix products, arithmetic and copies ran while one was open for 2% of the time, Pallas kernels for 0%

profile of v1, /device:TPU:0, one launch (start us, length us, event | category | flops | bytes accessed | tf_op | source)
XLA Modules:
  0.0 86.3 jit_solution(4747821130605971579)
XLA Ops:
  0.0 1.2 %sine_negate_fusion = (f32[384,1,192]{0,2,1:T(8,128)S(1)}, f32[384,1,192]{0,2,1:T(8,128)S(1)}) fusion(), kind=kLoop, calls=%fused_computation.30 | loop fusion | flops 737280 | bytes 589824 | tf_op jit(solution)/shard_map/neg | solution.py:94
  1.2 0.7 compare_select_fusion
  1.9 0.7 compare_select_fusion.1
  3.3 1.0 %gather_fusion = bf16[256,3,128]{2,1,0:T(4,128)(2,1)S(1)} fusion(bf16[32,3,128]{2,1,0:T(4,128)(2,1)S(1)} %bitcast.192, s32[1024]{0:T(1024)S(1)} %get-tuple-element.20), kind=kCustom, calls=%fused_computation | custom fusion | bytes 394240 | tf_op jit(solution)/shard_map/gather | solution.py:88
  4.3 4.4 %convolution_multiply_fusion.1 = f32[256,3,64]{2,1,0:T(4,128)S(1)} fusion(bf16[256,3,128]{2,1,0:T(4,128)(2,1)S(1)} %gather_fusion, bf16[256,64,128]{2,1,0:T(8,128)(2,1)} %param.6, f32[256]{0:T(256)S(1)} %compare_convert_fusion), kind=kOutput, calls=%fused_computation.5 | convolution fusion | flops 12632064 | bytes 4588544 | tf_op jit(solution)/shard_map/pcq,pnq->pcn/dot_general | solution.py:89
  8.8 8.3 %scatter_fusion = f32[96,3,64]{2,1,0:T(4,128)S(1)} fusion(f32[96,3,64]{2,1,0:T(4,128)S(1)} %broadcast_in_dim.24, s32[256]{0:T(256)S(1)} %copy-done.2, f32[256,3,64]{2,1,0:T(4,128)S(1)} %convolution_multiply_fusion.1), kind=kCustom, calls=%fused_computation.2 | custom fusion | flops 49152 | bytes 590848 | tf_op jit(solution)/shard_map/scatter-add | solution.py:91
  17.1 0.1 reshape.727
  17.2 0.9 convolution_bitcast_fusion.4
  18.1 0.8 copy.33
  18.9 2.5 %reshape.743 = f32[4,1,4608]{2,1,0:T(1,128)} reshape(f32[192,2,3,2,8]{4,3,2,1,0:T(2,128)S(1)} %bitcast.193) | data formatting | bytes 147456
  21.4 6.3 %all-to-all-start = ((f32[4,1,4608]{2,1,0:T(1,128)}), f32[4,1,4608]{2,1,0:T(1,128)S(1)}, u32[]{:S(2)}, u32[]{:S(2)}) async-start(f32[4,1,4608]{2,1,0:T(1,128)} %reshape.743), calls=%async_computation | async-start | bytes 147456 | tf_op jit(solution)/shard_map/all_to_all | solution.py:105
  28.6 4.9 %all-to-all-done = f32[4,1,4608]{2,1,0:T(1,128)S(1)} async-done(((f32[4,1,4608]{2,1,0:T(1,128)}), f32[4,1,4608]{2,1,0:T(1,128)S(1)}, u32[]{:S(2)}, u32[]{:S(2)}) %all-to-all-start) | async-done | bytes 73760 | tf_op jit(solution)/shard_map/all_to_all | solution.py:105
  33.5 0.5 broadcast.1152
  34.0 0.8 reduce
  34.8 1.8 %reshape.744 = f32[192,2,3,2,8]{4,3,2,1,0:T(2,128)S(1)} reshape(f32[4,4608]{1,0:T(4,128)S(1)} %reduce) | data formatting | bytes 147456
  36.6 0.7 copy.34
  37.3 0.4 convolution_bitcast_fusion.3
  37.9 0.9 reshape.745
  38.7 3.7 %all-to-all-start.1 = ((f32[8,1,2304]{2,1,0:T(1,128)}), f32[8,1,2304]{2,1,0:T(1,128)S(1)}, u32[]{:S(2)}, u32[]{:S(2)}) async-start(f32[8,1,2304]{2,1,0:T(1,128)} %reshape.745), calls=%async_computation.1 | async-start | bytes 147456 | tf_op jit(solution)/shard_map/all_to_all | solution.py:17
  42.4 5.1 %all-to-all-done.1 = f32[8,1,2304]{2,1,0:T(1,128)S(1)} async-done(((f32[8,1,2304]{2,1,0:T(1,128)}), f32[8,1,2304]{2,1,0:T(1,128)S(1)}, u32[]{:S(2)}, u32[]{:S(2)}) %all-to-all-start.1) | async-done | bytes 73760 | tf_op jit(solution)/shard_map/all_to_all | solution.py:17
  47.5 0.8 reduce.1
  48.3 0.2 reshape.746
  48.6 0.1 copy.35
  48.7 0.4 convolution_bitcast_fusion.2
  49.0 0.1 multiply_subtract_fusion.5
  49.1 0.1 multiply_subtract_fusion.2
  49.3 0.4 convolution_bitcast_fusion.1
  49.8 0.9 reshape.747
  50.6 3.4 %all-to-all-start.2 = ((f32[8,1,2304]{2,1,0:T(1,128)}), f32[8,1,2304]{2,1,0:T(1,128)S(1)}, u32[]{:S(2)}, u32[]{:S(2)}) async-start(f32[8,1,2304]{2,1,0:T(1,128)} %reshape.747), calls=%async_computation.2 | async-start | bytes 147456 | tf_op jit(solution)/shard_map/all_to_all | solution.py:116
  54.0 5.0 %all-to-all-done.2 = f32[8,1,2304]{2,1,0:T(1,128)S(1)} async-done(((f32[8,1,2304]{2,1,0:T(1,128)}), f32[8,1,2304]{2,1,0:T(1,128)S(1)}, u32[]{:S(2)}, u32[]{:S(2)}) %all-to-all-start.2) | async-done | bytes 73760 | tf_op jit(solution)/shard_map/all_to_all | solution.py:116
  59.0 0.8 reduce.2
  59.8 0.2 reshape.748
  60.0 0.4 convolution_bitcast_fusion
  60.4 0.2 copy.82
  60.6 0.9 %reshape.749 = f32[4,1,4608]{2,1,0:T(1,128)} reshape(f32[32,2,3,2,48]{4,3,2,1,0:T(2,128)S(1)} %bitcast.200) | data formatting | bytes 147456
  61.5 3.6 %all-to-all-start.3 = ((f32[4,1,4608]{2,1,0:T(1,128)}), f32[4,1,4608]{2,1,0:T(1,128)S(1)}, u32[]{:S(2)}, u32[]{:S(2)}) async-start(f32[4,1,4608]{2,1,0:T(1,128)} %reshape.749), calls=%async_computation.3 | async-start | bytes 147456 | tf_op jit(solution)/shard_map/all_to_all | solution.py:122
  65.2 1.2 %sine_multiply_fusion = (f32[1,192,384]{2,1,0:T(8,128)S(1)}, f32[1,192,384]{2,1,0:T(8,128)S(1)}) fusion(f32[192]{0:T(256)S(1)} %fusion.67, f32[192]{0:T(256)S(1)} %fusion.61), kind=kLoop, calls=%fused_computation.25 | loop fusion | flops 811008 | bytes 591360 | tf_op jit(solution)/shard_map/mul | solution.py:97
  66.4 4.3 %all-to-all-done.3 = f32[4,1,4608]{2,1,0:T(1,128)S(1)} async-done(((f32[4,1,4608]{2,1,0:T(1,128)}), f32[4,1,4608]{2,1,0:T(1,128)S(1)}, u32[]{:S(2)}, u32[]{:S(2)}) %all-to-all-start.3) | async-done | bytes 73760 | tf_op jit(solution)/shard_map/all_to_all | solution.py:122
  70.7 0.8 reduce.3
  71.5 0.3 reshape.750
  71.9 0.1 copy.80
  72.0 0.1 all_to_all.54
  72.2 0.5 fusion
  72.6 0.1 reshape.688
  72.8 1.0 %gather_fusion.1 = bf16[256,3,64]{2,1,0:T(4,128)(2,1)S(1)} fusion(bf16[96,3,64]{2,1,0:T(4,128)(2,1)S(1)} %bitcast.196, s32[1024]{0:T(1024)S(1)} %get-tuple-element.19), kind=kCustom, calls=%fused_computation.1 | custom fusion | bytes 197632 | tf_op jit(solution)/shard_map/gather | solution.py:127
  73.8 3.4 %convolution_multiply_fusion = f32[256,3,128]{2,1,0:T(4,128)S(1)} fusion(bf16[256,3,64]{2,1,0:T(4,128)(2,1)S(1)} %gather_fusion.1, bf16[256,64,128]{2,1,0:T(8,128)(2,1)} %param.6, f32[256]{0:T(256)S(1)} %compare_convert_fusion), kind=kOutput, calls=%fused_computation.4 | convolution fusion | flops 12681216 | bytes 4686848 | tf_op jit(solution)/shard_map/pcn,pnq->pcq/dot_general | solution.py:128
  77.2 8.4 %scatter_fusion.1 = f32[32,3,128]{2,1,0:T(4,128)S(1)} fusion(f32[32,3,128]{2,1,0:T(4,128)S(1)} %broadcast_in_dim.22, s32[256]{0:T(256)S(1)} %copy-done.3, f32[256,3,128]{2,1,0:T(4,128)S(1)} %convolution_multiply_fusion), kind=kCustom, calls=%fused_computation.3 | custom fusion | flops 98304 | bytes 1180672 | tf_op jit(solution)/shard_map/scatter-add | solution.py:132
  85.7 0.6 copy-done.1
  (47 shorter events, 1.2 us)
Async XLA Ops:
  0.0 3.3 %copy-start = (bf16[3,4096]{1,0:T(4,128)(2,1)S(1)}, bf16[3,4096]{1,0:T(4,128)(2,1)}, u32[]{:S(2)}) copy-start(bf16[3,4096]{1,0:T(4,128)(2,1)} %param.5) | copy-start | bytes 73732
  0.0 8.8 %copy-start.2 = (s32[256]{0:T(256)S(1)}, s32[256]{0:T(256)}, u32[]{:S(2)}) copy-start(s32[256]{0:T(256)} %param.8) | copy-start | bytes 3076
  21.4 12.1 %all-to-all-start = ((f32[4,1,4608]{2,1,0:T(1,128)}), f32[4,1,4608]{2,1,0:T(1,128)S(1)}, u32[]{:S(2)}, u32[]{:S(2)}) async-start(f32[4,1,4608]{2,1,0:T(1,128)} %reshape.743), calls=%async_computation | async-start | bytes 147456 | tf_op jit(solution)/shard_map/all_to_all | solution.py:105
  38.7 8.8 %all-to-all-start.1 = ((f32[8,1,2304]{2,1,0:T(1,128)}), f32[8,1,2304]{2,1,0:T(1,128)S(1)}, u32[]{:S(2)}, u32[]{:S(2)}) async-start(f32[8,1,2304]{2,1,0:T(1,128)} %reshape.745), calls=%async_computation.1 | async-start | bytes 147456 | tf_op jit(solution)/shard_map/all_to_all | solution.py:17
  50.6 8.4 %all-to-all-start.2 = ((f32[8,1,2304]{2,1,0:T(1,128)}), f32[8,1,2304]{2,1,0:T(1,128)S(1)}, u32[]{:S(2)}, u32[]{:S(2)}) async-start(f32[8,1,2304]{2,1,0:T(1,128)} %reshape.747), calls=%async_computation.2 | async-start | bytes 147456 | tf_op jit(solution)/shard_map/all_to_all | solution.py:116
  61.5 15.7 %copy-start.3 = (s32[256]{0:T(256)S(1)}, s32[256]{0:T(256)}, u32[]{:S(2)}) copy-start(s32[256]{0:T(256)} %param.7) | copy-start | bytes 3076
  61.5 9.2 %all-to-all-start.3 = ((f32[4,1,4608]{2,1,0:T(1,128)}), f32[4,1,4608]{2,1,0:T(1,128)S(1)}, u32[]{:S(2)}, u32[]{:S(2)}) async-start(f32[4,1,4608]{2,1,0:T(1,128)} %reshape.749), calls=%async_computation.3 | async-start | bytes 147456 | tf_op jit(solution)/shard_map/all_to_all | solution.py:122
  85.7 0.6 copy-start.1
